TPU v7x, 32 devices: a whole 2x2x4 slice. The times are simulated.
32 devices in a mesh: chan: 16 (over z, y, x), tm: 2 (over core).
Axes of the slice: x: 2, y: 2, z: 4, core: 2. Of those that a mesh axis runs over, the one named last changes fastest.
Arguments:
- signal: bfloat16 [1280, 16384], P('chan', 'tm'), may hold values from -6 to 6
- channel_mask: int32 [1280], P('chan'), may hold values 0 or 1
- seg_offsets: int32 [256], P('tm'), may hold values from 0 to 8191, as said below
- slow_steps: int32 [512], replicated, may hold values from -512 to 512
Outputs:
- beam: float32 [128, 2, 512, 256], P('chan', None, None, 'tm')
- power: float32 [512, 256], P('chan', 'tm')
Inputs may be any that keep to these rules, and one draw needn't show every extreme that they name: `seg_offsets`: entry s lies in [(s mod 128) * 64, (s mod 128) * 64 + 63]; some entry reaches the top of its interval.
All inputs are finite; a program needn't handle non-finite values. No bound on the sum of `channel_mask` on one device may be relied on, other than what follows from the above.
Results may differ from a plain program's by a relative error of at most 0.0048.
Values may be sent and summed in bfloat16 or wider, within the bound.
A program may use at most 64 MiB of HBM per device.

v0:
```python
import functools
import math

import jax
import jax.numpy as jnp
import ml_dtypes
import numpy as np
from jax import lax
from jax.experimental import pallas as pl
from jax.experimental.pallas import tpu as pltpu
from jax.sharding import PartitionSpec as P

SEG = 256
NF = 128
NP = 512
SUBSTEPS = 16
HOP = 64
LANES = 128
CHUNK = 16
ROWS = 64
VMEM_LIMIT = 60 * 1024 * 1024


def make_table():
    points = np.arange(SEG)
    bins = np.arange(1, NF + 1)
    taper = 0.5 - 0.5 * np.cos(2.0 * np.pi * points / SEG)
    angle = ((bins[:, None] * points[None, :]) % SEG) * (2.0 * np.pi / SEG)
    scale = 1.0 / math.sqrt(3.0 * SEG / 8.0)
    table = np.stack([taper * np.cos(angle), -taper * np.sin(angle)]).reshape(2, 2, NF // 2, SEG) * scale
    table = table.transpose(1, 0, 2, 3).reshape(2 * NF, SEG)
    return jnp.asarray(table.astype(np.float32).astype(ml_dtypes.bfloat16))


def turn(index):
    quarter = SEG * SUBSTEPS // 4
    quadrant = (index + quarter // 2) >> 10
    x = (index - quadrant * quarter).astype(jnp.float32) * (0.5 * math.pi / quarter)
    y = x * x
    sin = x * (1.0 + y * (-1.0 / 6 + y * (1.0 / 120 + y * (-1.0 / 5040 + y * (1.0 / 362880)))))
    cos = 1.0 + y * (-0.5 + y * (1.0 / 24 + y * (-1.0 / 720 + y * (1.0 / 40320))))
    odd = (quadrant & 1) == 1
    c, d = jnp.where(odd, sin, cos), jnp.where(odd, cos, sin)
    return jnp.where(((quadrant + 1) & 2) == 2, -c, c), jnp.where((quadrant & 2) == 2, -d, d)


def fused_kernel(offs, x_ref, mask_ref, table_ref, slow_ref, out_ref, power_ref, beam_ref, slow, held_signal, p0, p1, s0, s1, send, recv, steer, terms, arrived, send_sems, recv_sems, power_sems, halo_sems, out_sems, signal_sends, signal_recvs, *, ranks, blocks):
    chans = x_ref.shape[0]
    chunks = chans // CHUNK
    segs = p0.shape[0] // CHUNK
    own = NF // ranks
    slows = NP // ranks
    width = ranks * CHUNK
    total = chans * ranks
    modulus = SEG * SUBSTEPS
    me = lax.axis_index("chan")

    tm = lax.axis_index("tm")
    half = ranks // 2
    side = me // half
    mirror = (1 - side) * half + lax.rem(me, half)
    span = x_ref.shape[1]
    half_bins = NF // 2

    def peer(d):
        return lax.rem(side + 1 + d // half, 2) * half + lax.rem(me + d, half)

    barrier = pltpu.get_barrier_semaphore()
    mesh_ids = pl.DeviceIdType.MESH

    def greet(d, carry):
        pl.semaphore_signal(barrier, inc=1, device_id={"chan": peer(d)}, device_id_type=mesh_ids)
        return carry

    def others_of(body):
        lax.fori_loop(0, half, body, 0)
        lax.fori_loop(half + 1, ranks, body, 0)

    @pl.when(tm > 0)
    def _():
        pl.semaphore_signal(barrier, inc=1, device_id={"tm": tm - 1}, device_id_type=mesh_ids)

    @pl.when(tm < blocks - 1)
    def _():
        pl.semaphore_signal(barrier, inc=1, device_id={"tm": tm + 1}, device_id_type=mesh_ids)

    others_of(greet)

    def mask_rows(chunk, carry):
        rows = pl.ds(pl.multiple_of(chunk * CHUNK, CHUNK), CHUNK)
        mask = jnp.broadcast_to(mask_ref[rows, :], (CHUNK, LANES))

        def one(tile, carry):
            columns = pl.ds(pl.multiple_of(tile * LANES, LANES), LANES)
            held_signal[0, rows, columns] = (x_ref[rows, columns].astype(jnp.float32) * mask).astype(jnp.bfloat16)
            return carry

        return lax.fori_loop(0, span // LANES, one, carry, unroll=8)

    lax.fori_loop(0, chunks, mask_rows, 0)
    pl.semaphore_wait(barrier, ranks - 1 + jnp.where(tm > 0, 1, 0) + jnp.where(tm < blocks - 1, 1, 0))

    def halo_copy(to):
        return pltpu.make_async_remote_copy(
            src_ref=held_signal.at[0, :, pl.ds(0, SEG)],
            dst_ref=held_signal.at[0, :, pl.ds(span, SEG)],
            send_sem=halo_sems.at[0],
            recv_sem=halo_sems.at[1],
            device_id={"tm": to},
            device_id_type=mesh_ids,
        )

    def mirror_copy(rows, columns, send_sem, recv_sem):
        return pltpu.make_async_remote_copy(
            src_ref=held_signal.at[0, rows, columns],
            dst_ref=held_signal.at[1, rows, columns],
            send_sem=send_sem,
            recv_sem=recv_sem,
            device_id={"chan": mirror},
            device_id_type=mesh_ids,
        )

    def signal_copy(chunk):
        rows = pl.ds(pl.multiple_of(chunk * CHUNK, CHUNK), CHUNK)
        return mirror_copy(rows, pl.ds(0, span), signal_sends.at[chunk], signal_recvs.at[chunk])

    relay = mirror_copy(pl.ds(0, chans), pl.ds(span, SEG), halo_sems.at[2], halo_sems.at[3])

    @pl.when(tm > 0)
    def _():
        halo_copy(tm - 1).start()

    def send_signal(chunk, carry):
        signal_copy(chunk).start()
        return carry

    lax.fori_loop(0, chunks, send_signal, 0)

    @pl.when(tm == blocks - 1)
    def _():
        held_signal[0, :, span:] = jnp.zeros((chans, SEG), jnp.bfloat16)

    for block in range(NP // LANES):
        row = slow_ref[:, block * LANES:(block + 1) * LANES].astype(jnp.float32)
        across = lax.broadcasted_iota(jnp.int32, (LANES, LANES), 1)
        down = lax.broadcasted_iota(jnp.int32, (LANES, LANES), 0)
        column = jnp.sum(jnp.where(across == down, jnp.broadcast_to(row, (LANES, LANES)), 0.0), axis=1, keepdims=True)
        slow[block * LANES:(block + 1) * LANES, :] = jnp.broadcast_to(column, (LANES, LANES)).astype(jnp.int32)

    @pl.when(tm < blocks - 1)
    def _():
        halo_copy(tm + 1).wait_recv()

    relay.start()

    def block_copy(slot, chunk, origin, to):
        return pltpu.make_async_remote_copy(
            src_ref=send.at[slot, chunk, pl.ds(lax.rem(to, half) * own, own)],
            dst_ref=recv.at[chunk, origin],
            send_sem=send_sems.at[slot, chunk],
            recv_sem=recv_sems.at[chunk],
            device_id={"chan": to},
            device_id_type=mesh_ids,
        )

    def spectra(slot, chunk, origin):
        top = pl.multiple_of(chunk * CHUNK, CHUNK)

        def gather(s, carry):
            start = pl.multiple_of((s // 2) * LANES, LANES)
            back = LANES - (offs[s] - start)
            tiles = held_signal[slot, pl.ds(top, CHUNK), pl.ds(start, 3 * LANES)].astype(jnp.float32)
            a, b, c = [pltpu.roll(tiles[:, i * LANES:(i + 1) * LANES], back, 1) for i in range(3)]
            keep = lax.broadcasted_iota(jnp.int32, (CHUNK, LANES), 1) < back
            p0[pl.ds(s, CHUNK, stride=segs), :] = jnp.where(keep, a, b)
            p1[pl.ds(s, CHUNK, stride=segs), :] = jnp.where(keep, b, c)
            return carry

        lax.fori_loop(0, segs, gather, 0, unroll=16)
        table = table_ref[pl.ds(pl.multiple_of(side * NF, NF), NF), :]

        def transform(i, carry):
            rows = pl.ds(pl.multiple_of(i * 2 * segs, 2 * segs), 2 * segs)
            piece = jnp.concatenate([p0[rows, :], p1[rows, :]], axis=1).astype(jnp.bfloat16)
            spec = lax.dot_general(table, piece, (((1,), (1,)), ((), ())), preferred_element_type=jnp.float32)
            for part in range(2):
                both = spec[:, part * segs:(part + 1) * segs]
                s0[pl.ds(2 * i + part, half_bins, stride=CHUNK), :] = both[:half_bins]
                s1[pl.ds(2 * i + part, half_bins, stride=CHUNK), :] = both[half_bins:]
            return carry

        lax.fori_loop(0, CHUNK // 2, transform, 0, unroll=8)

        def pack(f, carry):
            rows = pl.ds(pl.multiple_of(f * CHUNK, CHUNK), CHUNK)
            send[slot, chunk, f] = jnp.concatenate([s0[rows, :], s1[rows, :]], axis=1).astype(jnp.bfloat16)
            return carry

        lax.fori_loop(0, half_bins, pack, 0, unroll=8)

        def launch(d, carry):
            block_copy(slot, chunk, origin, peer(d)).start()
            return carry

        lax.fori_loop(half + 1, ranks, launch, 0)
        recv[chunk, origin] = send[slot, chunk, pl.ds(lax.rem(me, half) * own, own)]

    def own_spectra(chunk, carry):
        spectra(0, chunk, me)
        return carry

    lax.fori_loop(0, chunks, own_spectra, 0)

    def steering(step, carry):
        f, rows = step // (NP // ROWS), lax.rem(step, NP // ROWS) * ROWS
        rows = pl.multiple_of(rows, ROWS)
        kp = (slow[pl.ds(rows, ROWS), :] * (me * own + f + 1)) & (modulus - 1)
        lane = lax.broadcasted_iota(jnp.int32, (ROWS, LANES), 1)
        first = (lane // CHUNK) * chans + (lane & (CHUNK - 1))
        scale = 1.0 / math.sqrt(total)
        cos0, sin0 = turn((kp * first) & (modulus - 1))
        cos0, sin0 = cos0 * scale, sin0 * scale
        hops = jnp.where(lane == 0, CHUNK, (LANES // CHUNK) * chans)
        cosp, sinp = turn((kp * hops) & (modulus - 1))
        rc, rs, bc, bs = [jnp.broadcast_to(v[:, i:i + 1], (ROWS, LANES)) for i in (0, 1) for v in (cosp, sinp)]
        for block in range(width // LANES):
            columns = slice(block * LANES, (block + 1) * LANES)
            cos, sin = cos0, sin0
            for chunk in range(chunks):
                steer[f, chunk, pl.ds(rows, ROWS), columns] = cos.astype(jnp.bfloat16)
                steer[f, chunk, pl.ds(NP + rows, ROWS), columns] = sin.astype(jnp.bfloat16)
                cos, sin = cos * rc - sin * rs, cos * rs + sin * rc
            cos0, sin0 = cos0 * bc - sin0 * bs, cos0 * bs + sin0 * bc
        return carry

    relay.wait_recv()
    steps = own * (NP // ROWS)

    def mirror_spectra(chunk, carry):
        lax.fori_loop(steps * chunk // (2 * chunks), steps * (chunk + 1) // (2 * chunks), steering, 0)
        signal_copy(chunk).wait_recv()
        spectra(1, chunk, mirror)
        return carry

    lax.fori_loop(0, chunks, mirror_spectra, 0)
    lax.fori_loop(steps // 2, steps, steering, 0)

    others = pl.ds(0, ranks - 1)

    def out_copy(f):
        return pltpu.make_async_copy(beam_ref.at[f], out_ref.at[f], out_sems.at[f])

    def add(chunk, first, last):
        held = recv.at[chunk, pl.ds(0, ranks - 2)]
        pltpu.make_async_copy(held, held, recv_sems.at[chunk]).wait()

        def one_bin(f, carry):
            spec = recv[chunk, :, f].reshape(width, 2 * segs)
            both = jnp.dot(steer[f, chunk], spec, preferred_element_type=jnp.float32)
            real = both[:NP, :segs] - both[NP:, segs:]
            imag = both[:NP, segs:] + both[NP:, :segs]
            beam_ref[f, 0] = real if first else beam_ref[f, 0] + real
            beam_ref[f, 1] = imag if first else beam_ref[f, 1] + imag
            if last:
                out_copy(f).start()
            return carry

        lax.fori_loop(0, own, one_bin, 0)

    add(0, True, False)

    def more(chunk, carry):
        add(chunk, False, False)
        return carry

    lax.fori_loop(1, chunks - 1, more, 0)
    add(chunks - 1, False, True)

    def power_copy(to):
        return pltpu.make_async_remote_copy(
            src_ref=terms.at[to],
            dst_ref=arrived.at[me],
            send_sem=power_sems.at[0],
            recv_sem=power_sems.at[1],
            device_id={"chan": to},
            device_id_type=pl.DeviceIdType.MESH,
        )

    def power_of(to):
        rows = pl.ds(pl.multiple_of(to * slows, slows), slows)

        def one_bin(f, acc):
            real, imag = beam_ref[f, 0, rows, :], beam_ref[f, 1, rows, :]
            return acc + (real * real + imag * imag)

        acc = lax.fori_loop(0, own, one_bin, jnp.zeros((slows, segs), jnp.float32), unroll=2)
        return acc * (1.0 / NF)

    def power_term(d, carry):
        to = peer(d)
        terms[to] = power_of(to).astype(terms.dtype)
        power_copy(to).start()
        return carry

    others_of(power_term)
    arrived[me] = power_of(me).astype(arrived.dtype)
    pltpu.make_async_copy(arrived.at[others], arrived.at[others], power_sems.at[1]).wait()

    def sum_up(r, acc):
        return acc + arrived[r].astype(jnp.float32)

    power_ref[...] = lax.fori_loop(0, ranks, sum_up, jnp.zeros((slows, segs), jnp.float32))

    def finish(chunk, carry):
        sent = recv.at[chunk, pl.ds(0, half - 1)]
        pltpu.make_async_copy(sent, sent, send_sems.at[0, chunk]).wait()
        pltpu.make_async_copy(sent, sent, send_sems.at[1, chunk]).wait()
        signal_copy(chunk).wait_send()
        return carry

    lax.fori_loop(0, chunks, finish, 0)
    pltpu.make_async_copy(terms.at[others], terms.at[others], power_sems.at[0]).wait()

    def written(f, carry):
        out_copy(f).wait()
        return carry

    lax.fori_loop(0, own, written, 0)

    relay.wait_send()

    @pl.when(tm > 0)
    def _():
        halo_copy(tm - 1).wait_send()


def fused(signal, mask, offsets, table, slow, ranks, blocks):
    chans, segs = signal.shape[0], offsets.shape[0]
    slows = NP // ranks
    term = jnp.bfloat16 if slows % 16 == 0 else jnp.float32
    own, chunks = NF // ranks, chans // CHUNK
    vmem = pl.BlockSpec(memory_space=pltpu.VMEM)
    return pl.pallas_call(
        functools.partial(fused_kernel, ranks=ranks, blocks=blocks),
        out_shape=(
            jax.ShapeDtypeStruct((own, 2, NP, segs), jnp.float32),
            jax.ShapeDtypeStruct((NP // ranks, segs), jnp.float32),
        ),
        in_specs=[pl.BlockSpec(memory_space=pltpu.SMEM), vmem, vmem, vmem, vmem],
        out_specs=(pl.BlockSpec(memory_space=pl.ANY), vmem),
        scratch_shapes=[
            pltpu.VMEM((own, 2, NP, segs), jnp.float32),
            pltpu.VMEM((NP, LANES), jnp.int32),
            pltpu.VMEM((2, chans, signal.shape[1] + SEG), jnp.bfloat16),
        ]
        + [pltpu.VMEM((CHUNK * segs, LANES), jnp.float32)] * 2
        + [pltpu.VMEM((NF // 2 * CHUNK, segs), jnp.float32)] * 2
        + [
            pltpu.VMEM((2, chunks, NF // 2, CHUNK, 2 * segs), jnp.bfloat16),
            pltpu.VMEM((chunks, ranks, own, CHUNK, 2 * segs), jnp.bfloat16),
            pltpu.VMEM((own, chunks, 2 * NP, ranks * CHUNK), jnp.bfloat16),
            pltpu.VMEM((ranks, slows, segs), term),
            pltpu.VMEM((ranks, slows, segs), term),
            pltpu.SemaphoreType.DMA((2, chunks)),
            pltpu.SemaphoreType.DMA((chunks,)),
            pltpu.SemaphoreType.DMA((2,)),
            pltpu.SemaphoreType.DMA((4,)),
            pltpu.SemaphoreType.DMA((own,)),
            pltpu.SemaphoreType.DMA((chunks,)),
            pltpu.SemaphoreType.DMA((chunks,)),
        ],
        compiler_params=pltpu.CompilerParams(vmem_limit_bytes=VMEM_LIMIT, collective_id=0, has_side_effects=True),
        cost_estimate=pl.CostEstimate(flops=7 << 30, bytes_accessed=8 << 20, transcendentals=0),
        name="beamform",
    )(offsets, signal, mask, table, slow)


def local(signal, channel_mask, seg_offsets, slow_steps):
    mask = channel_mask[:, None].astype(jnp.float32)
    ranks, blocks = lax.axis_size("chan"), lax.axis_size("tm")
    return fused(signal, mask, seg_offsets, make_table(), slow_steps[None, :], ranks, blocks)


def solution(mesh):
    in_specs = (P("chan", "tm"), P("chan"), P("tm"), P())
    out_specs = (P("chan", None, None, "tm"), P("chan", "tm"))
    return jax.shard_map(local, mesh=mesh, in_specs=in_specs, out_specs=out_specs, check_vma=False)
```

profile of v0, /device:TPU:0, one launch (start us, length us, event | category | flops | bytes accessed | tf_op | source)
XLA Modules:
  0.0 124.0 jit_solution(7752187408546634160)
XLA Ops:
  0.6 0.7 convert_bitcast_fusion
  1.3 0.7 copy.7.mask_ref
  2.0 116.7 %beamform.1 = (f32[8,2,512,128]{3,2,1,0:T(8,128)}, f32[32,128]{1,0:T(8,128)}) custom-call(s32[128]{0:T(128)} %offs.1, bf16[80,8192]{1,0:T(8,128)(2,1)} %x_ref.1, f32[80,1]{1,0:T(8,128)} %copy.7.mask_ref, bf16[256,256]{1,0:T(8,128)(2,1)} %constant.2.clone.table_ref, s32[1,512]{1,0:T(1,128)} %bitcast.3), custom_call_target="tpu_custom_call" | custom-call | flops 7516192768 | bytes 8388608 | tf_op jit(solution)/shard_map/beamform/pallas_call | solution.py:343
  118.7 0.0 copy-start
  118.7 4.6 %copy.10 = f32[8,2,512,128]{3,2,1,0:T(8,128)} copy(f32[8,2,512,128]{3,2,1,0:T(8,128)} %get-tuple-element.4) | data formatting | bytes 8388608
  123.3 0.0 copy-done
  123.3 0.6 copy.11
Async XLA Ops:
  118.7 4.6 %copy-start = (f32[32,128]{1,0:T(8,128)S(1)}, f32[32,128]{1,0:T(8,128)}, u32[]{:S(2)}) copy-start(f32[32,128]{1,0:T(8,128)} %get-tuple-element.5) | copy-start | bytes 49156
where the time goes:
time: 124 us
  Pallas kernels  117 us (94%)
  local copies, waits for them, and re-layouts  5.94 us (5%)
    pallas_call x1, Pallas kernels, fused(): pl.pallas_call(functools.partial(fused_kernel, ranks=ranks, blocks=blocks...  117 us
    unnamed x4, local copies, waits for them, and re-layouts  5.22 us

commit v1 on v0

--- a/solution.py
+++ b/solution.py
@@ -18,7 +18,7 @@
 LANES = 128
 CHUNK = 16
 ROWS = 64
-VMEM_LIMIT = 60 * 1024 * 1024
+VMEM_LIMIT = 46 * 1024 * 1024
 
 
 def make_table():
@@ -44,7 +44,7 @@
     return jnp.where(((quadrant + 1) & 2) == 2, -c, c), jnp.where((quadrant & 2) == 2, -d, d)
 
 
-def fused_kernel(offs, x_ref, mask_ref, table_ref, slow_ref, out_ref, power_ref, beam_ref, slow, held_signal, p0, p1, s0, s1, send, recv, steer, terms, arrived, send_sems, recv_sems, power_sems, halo_sems, out_sems, signal_sends, signal_recvs, *, ranks, blocks):
+def fused_kernel(offs, x_ref, mask_ref, table_ref, slow_ref, beam_ref, power_ref, slow, held_signal, p0, p1, s0, s1, send, recv, steer, terms, arrived, send_sems, recv_sems, power_sems, halo_sems, signal_sends, signal_recvs, *, ranks, blocks):
     chans = x_ref.shape[0]
     chunks = chans // CHUNK
     segs = p0.shape[0] // CHUNK
@@ -63,7 +63,7 @@
     half_bins = NF // 2
 
     def peer(d):
-        return lax.rem(side + 1 + d // half, 2) * half + lax.rem(me + d, half)
+        return (1 - side + d // half) % 2 * half + ((me % half) ^ (d % half))
 
     barrier = pltpu.get_barrier_semaphore()
     mesh_ids = pl.DeviceIdType.MESH
@@ -88,7 +88,11 @@
 
     def mask_rows(chunk, carry):
         rows = pl.ds(pl.multiple_of(chunk * CHUNK, CHUNK), CHUNK)
-        mask = jnp.broadcast_to(mask_ref[rows, :], (CHUNK, LANES))
+        across = lax.broadcasted_iota(jnp.int32, (CHUNK, chans), 1)
+        down = lax.broadcasted_iota(jnp.int32, (CHUNK, chans), 0) + chunk * CHUNK
+        live = jnp.broadcast_to(mask_ref[...].astype(jnp.float32), (CHUNK, chans))
+        mask = jnp.sum(jnp.where(across == down, live, 0.0), axis=1, keepdims=True)
+        mask = jnp.broadcast_to(mask, (CHUNK, LANES))
 
         def one(tile, carry):
             columns = pl.ds(pl.multiple_of(tile * LANES, LANES), LANES)
@@ -134,7 +138,7 @@
         signal_copy(chunk).start()
         return carry
 
-    lax.fori_loop(0, chunks, send_signal, 0)
+    lax.fori_loop(0, 2, send_signal, 0)
 
     @pl.when(tm == blocks - 1)
     def _():
@@ -199,7 +203,7 @@
         lax.fori_loop(0, half_bins, pack, 0, unroll=8)
 
         def launch(d, carry):
-            block_copy(slot, chunk, origin, peer(d)).start()
+            block_copy(slot, chunk, origin, peer(ranks + half - d)).start()
             return carry
 
         lax.fori_loop(half + 1, ranks, launch, 0)
@@ -238,6 +242,12 @@
 
     def mirror_spectra(chunk, carry):
         lax.fori_loop(steps * chunk // (2 * chunks), steps * (chunk + 1) // (2 * chunks), steering, 0)
+        signal_copy(chunk).wait_send()
+
+        @pl.when(chunk + 2 < chunks)
+        def _():
+            signal_copy(chunk + 2).start()
+
         signal_copy(chunk).wait_recv()
         spectra(1, chunk, mirror)
         return carry
@@ -246,9 +256,6 @@
     lax.fori_loop(steps // 2, steps, steering, 0)
 
     others = pl.ds(0, ranks - 1)
-
-    def out_copy(f):
-        return pltpu.make_async_copy(beam_ref.at[f], out_ref.at[f], out_sems.at[f])
 
     def add(chunk, first, last):
         held = recv.at[chunk, pl.ds(0, ranks - 2)]
@@ -261,8 +268,6 @@
             imag = both[:NP, segs:] + both[NP:, :segs]
             beam_ref[f, 0] = real if first else beam_ref[f, 0] + real
             beam_ref[f, 1] = imag if first else beam_ref[f, 1] + imag
-            if last:
-                out_copy(f).start()
             return carry
 
         lax.fori_loop(0, own, one_bin, 0)
@@ -315,17 +320,10 @@
         sent = recv.at[chunk, pl.ds(0, half - 1)]
         pltpu.make_async_copy(sent, sent, send_sems.at[0, chunk]).wait()
         pltpu.make_async_copy(sent, sent, send_sems.at[1, chunk]).wait()
-        signal_copy(chunk).wait_send()
         return carry
 
     lax.fori_loop(0, chunks, finish, 0)
     pltpu.make_async_copy(terms.at[others], terms.at[others], power_sems.at[0]).wait()
-
-    def written(f, carry):
-        out_copy(f).wait()
-        return carry
-
-    lax.fori_loop(0, own, written, 0)
 
     relay.wait_send()
 
@@ -343,13 +341,12 @@
     return pl.pallas_call(
         functools.partial(fused_kernel, ranks=ranks, blocks=blocks),
         out_shape=(
-            jax.ShapeDtypeStruct((own, 2, NP, segs), jnp.float32),
-            jax.ShapeDtypeStruct((NP // ranks, segs), jnp.float32),
+            pltpu.VMEM((own, 2, NP, segs), jnp.float32),
+            pltpu.VMEM((NP // ranks, segs), jnp.float32),
         ),
         in_specs=[pl.BlockSpec(memory_space=pltpu.SMEM), vmem, vmem, vmem, vmem],
-        out_specs=(pl.BlockSpec(memory_space=pl.ANY), vmem),
+        out_specs=(vmem, vmem),
         scratch_shapes=[
-            pltpu.VMEM((own, 2, NP, segs), jnp.float32),
             pltpu.VMEM((NP, LANES), jnp.int32),
             pltpu.VMEM((2, chans, signal.shape[1] + SEG), jnp.bfloat16),
         ]
@@ -365,20 +362,18 @@
             pltpu.SemaphoreType.DMA((chunks,)),
             pltpu.SemaphoreType.DMA((2,)),
             pltpu.SemaphoreType.DMA((4,)),
-            pltpu.SemaphoreType.DMA((own,)),
             pltpu.SemaphoreType.DMA((chunks,)),
             pltpu.SemaphoreType.DMA((chunks,)),
         ],
         compiler_params=pltpu.CompilerParams(vmem_limit_bytes=VMEM_LIMIT, collective_id=0, has_side_effects=True),
         cost_estimate=pl.CostEstimate(flops=7 << 30, bytes_accessed=8 << 20, transcendentals=0),
         name="beamform",
-    )(offsets, signal, mask, table, slow)
+    )(*[pltpu.with_memory_space_constraint(x, pltpu.HBM) for x in (offsets, signal, mask, table, slow)])
 
 
 def local(signal, channel_mask, seg_offsets, slow_steps):
-    mask = channel_mask[:, None].astype(jnp.float32)
     ranks, blocks = lax.axis_size("chan"), lax.axis_size("tm")
-    return fused(signal, mask, seg_offsets, make_table(), slow_steps[None, :], ranks, blocks)
+    return fused(signal, channel_mask[None, :], seg_offsets, make_table(), slow_steps[None, :], ranks, blocks)
 
 
 def solution(mesh):

time: 124 us -> 110 us (0.89)
  Pallas kernels: 117 us -> 106 us
  local copies, waits for them, and re-layouts: 5.94 us -> 2.62 us
    pallas_call x1, Pallas kernels: 117 us -> 106 us  [fused(): pl.pallas_call(functools.partial(fused_kernel, ranks=ranks, blocks=blocks...]
    unnamed x4 -> x2, local copies, waits for them, and re-layouts: 5.22 us -> 2.62 us
where the time goes in v1:
time: 110 us
  Pallas kernels  106 us (96%)
  local copies, waits for them, and re-layouts  2.62 us (2%)
    pallas_call x1, Pallas kernels, fused(): pl.pallas_call(functools.partial(fused_kernel, ranks=ranks, blocks=blocks...  106 us
    unnamed x2, local copies, waits for them, and re-layouts  2.62 us

profile of v1, /device:TPU:0, one launch (start us, length us, event | category | flops | bytes accessed | tf_op | source)
XLA Modules:
  0.0 109.6 jit_solution(6288757040378274906)
XLA Ops:
  0.6 106.4 %beamform.1 = (f32[8,2,512,128]{3,2,1,0:T(8,128)S(1)}, f32[32,128]{1,0:T(8,128)S(1)}) custom-call(s32[128]{0:T(128)} %offs.1, bf16[80,8192]{1,0:T(8,128)(2,1)} %x_ref.1, s32[1,80]{1,0:T(1,128)} %bitcast.3, bf16[256,256]{1,0:T(8,128)(2,1)} %constant.2.clone.table_ref, s32[1,512]{1,0:T(1,128)} %bitcast.2), custom_call_target="tpu_custom_call" | custom-call | flops 7516192768 | bytes 8388608 | tf_op jit(solution)/shard_map/beamform/pallas_call | solution.py:341
  107.0 2.0 %copy.9 = f32[8,2,512,128]{3,2,1,0:T(8,128)} copy(f32[8,2,512,128]{3,2,1,0:T(8,128)S(1)} %get-tuple-element.2) | data formatting | bytes 8388608
  109.0 0.6 copy.10

commit v2 on v1

--- a/solution.py
+++ b/solution.py
@@ -18,6 +18,7 @@
 LANES = 128
 CHUNK = 16
 ROWS = 64
+PAD = 8
 VMEM_LIMIT = 46 * 1024 * 1024
 
 
@@ -44,10 +45,11 @@
     return jnp.where(((quadrant + 1) & 2) == 2, -c, c), jnp.where((quadrant & 2) == 2, -d, d)
 
 
-def fused_kernel(offs, x_ref, mask_ref, table_ref, slow_ref, beam_ref, power_ref, slow, held_signal, p0, p1, s0, s1, send, recv, steer, terms, arrived, send_sems, recv_sems, power_sems, halo_sems, signal_sends, signal_recvs, *, ranks, blocks):
+def fused_kernel(offs, x_ref, mask_ref, table_ref, slow_ref, beam_ref, power_ref, slow, held_signal, p0, p1, s0, s1, send, recv, steer, energy, terms, arrived, send_sems, recv_sems, power_sems, halo_sems, signal_sends, signal_recvs, edge_sends, edge_recvs, *, ranks, blocks):
     chans = x_ref.shape[0]
     chunks = chans // CHUNK
-    segs = p0.shape[0] // CHUNK
+    step = p0.shape[0] // CHUNK
+    segs = step - PAD
     own = NF // ranks
     slows = NP // ranks
     width = ranks * CHUNK
@@ -114,35 +116,41 @@
             device_id_type=mesh_ids,
         )
 
-    def mirror_copy(rows, columns, send_sem, recv_sem):
+    def signal_copy(chunk):
+        rows = pl.ds(pl.multiple_of(chunk * CHUNK, CHUNK), CHUNK)
         return pltpu.make_async_remote_copy(
-            src_ref=held_signal.at[0, rows, columns],
-            dst_ref=held_signal.at[1, rows, columns],
-            send_sem=send_sem,
-            recv_sem=recv_sem,
+            src_ref=held_signal.at[0, rows, pl.ds(0, span)],
+            dst_ref=held_signal.at[1, rows, pl.ds(0, span)],
+            send_sem=signal_sends.at[chunk],
+            recv_sem=signal_recvs.at[chunk],
             device_id={"chan": mirror},
             device_id_type=mesh_ids,
         )
 
-    def signal_copy(chunk):
+    def edge_copy(chunk, to):
         rows = pl.ds(pl.multiple_of(chunk * CHUNK, CHUNK), CHUNK)
-        return mirror_copy(rows, pl.ds(0, span), signal_sends.at[chunk], signal_recvs.at[chunk])
-
-    relay = mirror_copy(pl.ds(0, chans), pl.ds(span, SEG), halo_sems.at[2], halo_sems.at[3])
-
-    @pl.when(tm > 0)
-    def _():
-        halo_copy(tm - 1).start()
+        return pltpu.make_async_remote_copy(
+            src_ref=held_signal.at[1, rows, pl.ds(0, SEG)],
+            dst_ref=held_signal.at[1, rows, pl.ds(span, SEG)],
+            send_sem=edge_sends.at[chunk],
+            recv_sem=edge_recvs.at[chunk],
+            device_id={"tm": to},
+            device_id_type=mesh_ids,
+        )
 
     def send_signal(chunk, carry):
         signal_copy(chunk).start()
         return carry
 
+    @pl.when(tm > 0)
+    def _():
+        halo_copy(tm - 1).start()
+
     lax.fori_loop(0, 2, send_signal, 0)
 
     @pl.when(tm == blocks - 1)
     def _():
-        held_signal[0, :, span:] = jnp.zeros((chans, SEG), jnp.bfloat16)
+        held_signal[:, :, span:] = jnp.zeros((2, chans, SEG), jnp.bfloat16)
 
     for block in range(NP // LANES):
         row = slow_ref[:, block * LANES:(block + 1) * LANES].astype(jnp.float32)
@@ -154,8 +162,6 @@
     @pl.when(tm < blocks - 1)
     def _():
         halo_copy(tm + 1).wait_recv()
-
-    relay.start()
 
     def block_copy(slot, chunk, origin, to):
         return pltpu.make_async_remote_copy(
@@ -176,27 +182,27 @@
             tiles = held_signal[slot, pl.ds(top, CHUNK), pl.ds(start, 3 * LANES)].astype(jnp.float32)
             a, b, c = [pltpu.roll(tiles[:, i * LANES:(i + 1) * LANES], back, 1) for i in range(3)]
             keep = lax.broadcasted_iota(jnp.int32, (CHUNK, LANES), 1) < back
-            p0[pl.ds(s, CHUNK, stride=segs), :] = jnp.where(keep, a, b)
-            p1[pl.ds(s, CHUNK, stride=segs), :] = jnp.where(keep, b, c)
-            return carry
-
-        lax.fori_loop(0, segs, gather, 0, unroll=16)
+            p0[pl.ds(s, CHUNK, stride=step), :] = jnp.where(keep, a, b)
+            p1[pl.ds(s, CHUNK, stride=step), :] = jnp.where(keep, b, c)
+            return carry
+
+        lax.fori_loop(0, segs, gather, 0, unroll=128)
         table = table_ref[pl.ds(pl.multiple_of(side * NF, NF), NF), :]
 
         def transform(i, carry):
-            rows = pl.ds(pl.multiple_of(i * 2 * segs, 2 * segs), 2 * segs)
-            piece = jnp.concatenate([p0[rows, :], p1[rows, :]], axis=1).astype(jnp.bfloat16)
+            pair = [pl.ds(pl.multiple_of((2 * i + part) * step, 8), segs) for part in range(2)]
+            piece = jnp.concatenate([jnp.concatenate([p0[rows, :], p1[rows, :]], axis=1) for rows in pair]).astype(jnp.bfloat16)
             spec = lax.dot_general(table, piece, (((1,), (1,)), ((), ())), preferred_element_type=jnp.float32)
             for part in range(2):
                 both = spec[:, part * segs:(part + 1) * segs]
-                s0[pl.ds(2 * i + part, half_bins, stride=CHUNK), :] = both[:half_bins]
-                s1[pl.ds(2 * i + part, half_bins, stride=CHUNK), :] = both[half_bins:]
+                s0[pl.ds(2 * i + part, half_bins, stride=CHUNK + 8), :] = both[:half_bins]
+                s1[pl.ds(2 * i + part, half_bins, stride=CHUNK + 8), :] = both[half_bins:]
             return carry
 
         lax.fori_loop(0, CHUNK // 2, transform, 0, unroll=8)
 
         def pack(f, carry):
-            rows = pl.ds(pl.multiple_of(f * CHUNK, CHUNK), CHUNK)
+            rows = pl.ds(pl.multiple_of(f * (CHUNK + 8), 8), CHUNK)
             send[slot, chunk, f] = jnp.concatenate([s0[rows, :], s1[rows, :]], axis=1).astype(jnp.bfloat16)
             return carry
 
@@ -237,7 +243,6 @@
             cos0, sin0 = cos0 * bc - sin0 * bs, cos0 * bs + sin0 * bc
         return carry
 
-    relay.wait_recv()
     steps = own * (NP // ROWS)
 
     def mirror_spectra(chunk, carry):
@@ -249,6 +254,15 @@
             signal_copy(chunk + 2).start()
 
         signal_copy(chunk).wait_recv()
+
+        @pl.when(tm > 0)
+        def _():
+            edge_copy(chunk, tm - 1).start()
+
+        @pl.when(tm < blocks - 1)
+        def _():
+            edge_copy(chunk, tm + 1).wait_recv()
+
         spectra(1, chunk, mirror)
         return carry
 
@@ -266,11 +280,15 @@
             both = jnp.dot(steer[f, chunk], spec, preferred_element_type=jnp.float32)
             real = both[:NP, :segs] - both[NP:, segs:]
             imag = both[:NP, segs:] + both[NP:, :segs]
-            beam_ref[f, 0] = real if first else beam_ref[f, 0] + real
-            beam_ref[f, 1] = imag if first else beam_ref[f, 1] + imag
-            return carry
-
-        lax.fori_loop(0, own, one_bin, 0)
+            if not first:
+                real, imag = beam_ref[f, 0] + real, beam_ref[f, 1] + imag
+            beam_ref[f, 0] = real
+            beam_ref[f, 1] = imag
+            if last:
+                energy[...] += real * real + imag * imag
+            return carry
+
+        lax.fori_loop(0, own, one_bin, 0, unroll=8)
 
     add(0, True, False)
 
@@ -279,6 +297,7 @@
         return carry
 
     lax.fori_loop(1, chunks - 1, more, 0)
+    energy[...] = jnp.zeros((NP, segs), jnp.float32)
     add(chunks - 1, False, True)
 
     def power_copy(to):
@@ -294,12 +313,7 @@
     def power_of(to):
         rows = pl.ds(pl.multiple_of(to * slows, slows), slows)
 
-        def one_bin(f, acc):
-            real, imag = beam_ref[f, 0, rows, :], beam_ref[f, 1, rows, :]
-            return acc + (real * real + imag * imag)
-
-        acc = lax.fori_loop(0, own, one_bin, jnp.zeros((slows, segs), jnp.float32), unroll=2)
-        return acc * (1.0 / NF)
+        return energy[rows, :] * (1.0 / NF)
 
     def power_term(d, carry):
         to = peer(d)
@@ -320,12 +334,15 @@
         sent = recv.at[chunk, pl.ds(0, half - 1)]
         pltpu.make_async_copy(sent, sent, send_sems.at[0, chunk]).wait()
         pltpu.make_async_copy(sent, sent, send_sems.at[1, chunk]).wait()
+
+        @pl.when(tm > 0)
+        def _():
+            edge_copy(chunk, tm - 1).wait_send()
+
         return carry
 
     lax.fori_loop(0, chunks, finish, 0)
     pltpu.make_async_copy(terms.at[others], terms.at[others], power_sems.at[0]).wait()
-
-    relay.wait_send()
 
     @pl.when(tm > 0)
     def _():
@@ -350,18 +367,21 @@
             pltpu.VMEM((NP, LANES), jnp.int32),
             pltpu.VMEM((2, chans, signal.shape[1] + SEG), jnp.bfloat16),
         ]
-        + [pltpu.VMEM((CHUNK * segs, LANES), jnp.float32)] * 2
-        + [pltpu.VMEM((NF // 2 * CHUNK, segs), jnp.float32)] * 2
+        + [pltpu.VMEM((CHUNK * (segs + PAD), LANES), jnp.float32)] * 2
+        + [pltpu.VMEM((NF // 2 * (CHUNK + 8), segs), jnp.float32)] * 2
         + [
             pltpu.VMEM((2, chunks, NF // 2, CHUNK, 2 * segs), jnp.bfloat16),
             pltpu.VMEM((chunks, ranks, own, CHUNK, 2 * segs), jnp.bfloat16),
             pltpu.VMEM((own, chunks, 2 * NP, ranks * CHUNK), jnp.bfloat16),
+            pltpu.VMEM((NP, segs), jnp.float32),
             pltpu.VMEM((ranks, slows, segs), term),
             pltpu.VMEM((ranks, slows, segs), term),
             pltpu.SemaphoreType.DMA((2, chunks)),
             pltpu.SemaphoreType.DMA((chunks,)),
             pltpu.SemaphoreType.DMA((2,)),
-            pltpu.SemaphoreType.DMA((4,)),
+            pltpu.SemaphoreType.DMA((2,)),
+            pltpu.SemaphoreType.DMA((chunks,)),
+            pltpu.SemaphoreType.DMA((chunks,)),
             pltpu.SemaphoreType.DMA((chunks,)),
             pltpu.SemaphoreType.DMA((chunks,)),
         ],
@@ -371,9 +391,38 @@
     )(*[pltpu.with_memory_space_constraint(x, pltpu.HBM) for x in (offsets, signal, mask, table, slow)])
 
 
+def store_kernel(beam_ref, power_ref, beam_out, power_out, sems):
+    bins = beam_ref.shape[0]
+
+    def copy(f):
+        return pltpu.make_async_copy(beam_ref.at[f], beam_out.at[f], sems.at[f])
+
+    last = pltpu.make_async_copy(power_ref, power_out, sems.at[bins])
+    for f in range(bins):
+        copy(f).start()
+    last.start()
+    for f in range(bins):
+        copy(f).wait()
+    last.wait()
+
+
+def store(beam, power):
+    vmem, anywhere = pl.BlockSpec(memory_space=pltpu.VMEM), pl.BlockSpec(memory_space=pl.ANY)
+    return pl.pallas_call(
+        store_kernel,
+        out_shape=(jax.ShapeDtypeStruct(beam.shape, beam.dtype), jax.ShapeDtypeStruct(power.shape, power.dtype)),
+        in_specs=[vmem, vmem],
+        out_specs=(anywhere, anywhere),
+        scratch_shapes=[pltpu.SemaphoreType.DMA((beam.shape[0] + 1,))],
+        cost_estimate=pl.CostEstimate(flops=0, bytes_accessed=2 * beam.size * 4, transcendentals=0),
+        compiler_params=pltpu.CompilerParams(vmem_limit_bytes=8 << 20),
+        name="store",
+    )(*[pltpu.with_memory_space_constraint(x, pltpu.VMEM) for x in (beam, power)])
+
+
 def local(signal, channel_mask, seg_offsets, slow_steps):
     ranks, blocks = lax.axis_size("chan"), lax.axis_size("tm")
-    return fused(signal, channel_mask[None, :], seg_offsets, make_table(), slow_steps[None, :], ranks, blocks)
+    return store(*fused(signal, channel_mask[None, :], seg_offsets, make_table(), slow_steps[None, :], ranks, blocks))
 
 
 def solution(mesh):

time: 110 us -> 103 us (0.936)
  Pallas kernels: 106 us -> 102 us
  local copies, waits for them, and re-layouts: 2.62 us -> 0 us
    pallas_call x1, Pallas kernels: 106 us -> 100 us  [fused(): pl.pallas_call(functools.partial(fused_kernel, ranks=ranks, blocks=blocks...]
    unnamed x2 -> x0, local copies, waits for them, and re-layouts: 2.62 us -> none
    pallas_call x0 -> x1, Pallas kernels: none -> 2.08 us  [store(): pl.pallas_call(store_kernel, out_shape=(jax.ShapeDtypeStruct(beam.shape,...]
where the time goes in v2:
time: 103 us
  Pallas kernels  102 us (99%)
    pallas_call x1, Pallas kernels, fused(): pl.pallas_call(functools.partial(fused_kernel, ranks=ranks, blocks=blocks...  100 us
    pallas_call x1, Pallas kernels, store(): pl.pallas_call(store_kernel, out_shape=(jax.ShapeDtypeStruct(beam.shape,...  2.08 us

profile of v2, /device:TPU:0, one launch (start us, length us, event | category | flops | bytes accessed | tf_op | source)
XLA Modules:
  0.0 103.0 jit_solution(12597378550672330907)
XLA Ops:
  0.6 100.3 %beamform.1 = (f32[8,2,512,128]{3,2,1,0:T(8,128)S(1)}, f32[32,128]{1,0:T(8,128)S(1)}) custom-call(s32[128]{0:T(128)} %offs.1, bf16[80,8192]{1,0:T(8,128)(2,1)} %x_ref.1, s32[1,80]{1,0:T(1,128)} %bitcast.3, bf16[256,256]{1,0:T(8,128)(2,1)} %constant.2.clone.table_ref, s32[1,512]{1,0:T(1,128)} %bitcast.2), custom_call_target="tpu_custom_call" | custom-call | flops 7516192768 | bytes 8388608 | tf_op jit(solution)/shard_map/beamform/pallas_call | solution.py:358
  100.9 2.1 %store.1 = (f32[8,2,512,128]{3,2,1,0:T(8,128)}, f32[32,128]{1,0:T(8,128)}) custom-call(f32[8,2,512,128]{3,2,1,0:T(8,128)S(1)} %get-tuple-element.4.beam_ref, f32[32,128]{1,0:T(8,128)S(1)} %get-tuple-element.5.power_ref), custom_call_target="tpu_custom_call" | custom-call | bytes 8388608 | tf_op jit(solution)/shard_map/store/pallas_call | solution.py:411

commit v3 on v2

--- a/solution.py
+++ b/solution.py
@@ -45,8 +45,8 @@
     return jnp.where(((quadrant + 1) & 2) == 2, -c, c), jnp.where((quadrant & 2) == 2, -d, d)
 
 
-def fused_kernel(offs, x_ref, mask_ref, table_ref, slow_ref, beam_ref, power_ref, slow, held_signal, p0, p1, s0, s1, send, recv, steer, energy, terms, arrived, send_sems, recv_sems, power_sems, halo_sems, signal_sends, signal_recvs, edge_sends, edge_recvs, *, ranks, blocks):
-    chans = x_ref.shape[0]
+def fused_kernel(offsets_ref, signal_ref, channel_mask_ref, taper_ref, steps_ref, beam_ref, power_ref, offs, mask_ref, table_ref, slow_ref, x_ref, slow, held_signal, p0, p1, s0, s1, send, recv, steer, energy, terms, arrived, send_sems, recv_sems, power_sems, halo_sems, signal_sends, signal_recvs, edge_sends, edge_recvs, load_sems, small_sems, *, ranks, blocks):
+    chans = signal_ref.shape[0]
     chunks = chans // CHUNK
     step = p0.shape[0] // CHUNK
     segs = step - PAD
@@ -61,7 +61,7 @@
     half = ranks // 2
     side = me // half
     mirror = (1 - side) * half + lax.rem(me, half)
-    span = x_ref.shape[1]
+    span = signal_ref.shape[1]
     half_bins = NF // 2
 
     def peer(d):
@@ -70,13 +70,24 @@
     barrier = pltpu.get_barrier_semaphore()
     mesh_ids = pl.DeviceIdType.MESH
 
+    smalls = ((channel_mask_ref, mask_ref), (taper_ref, table_ref), (offsets_ref, offs), (steps_ref, slow_ref))
+    load_mask, load_table, load_offsets, load_steps = [pltpu.make_async_copy(*pair, small_sems.at[i]) for i, pair in enumerate(smalls)]
+    load_mask.start()
+    for chunk in range(chunks):
+        rows = pl.ds(chunk * CHUNK, CHUNK)
+        pltpu.make_async_copy(signal_ref.at[rows], x_ref.at[rows], load_sems.at[chunk]).start()
+
+    load_table.start()
+    load_offsets.start()
+    load_steps.start()
+
     def greet(d, carry):
         pl.semaphore_signal(barrier, inc=1, device_id={"chan": peer(d)}, device_id_type=mesh_ids)
         return carry
 
     def others_of(body):
-        lax.fori_loop(0, half, body, 0)
-        lax.fori_loop(half + 1, ranks, body, 0)
+        lax.fori_loop(0, half, body, 0, unroll=8)
+        lax.fori_loop(half + 1, ranks, body, 0, unroll=min(7, half - 1))
 
     @pl.when(tm > 0)
     def _():
@@ -88,22 +99,28 @@
 
     others_of(greet)
 
+    def load(chunk):
+        rows = pl.ds(pl.multiple_of(chunk * CHUNK, CHUNK), CHUNK)
+        return pltpu.make_async_copy(signal_ref.at[rows], x_ref.at[rows], load_sems.at[chunk])
+
     def mask_rows(chunk, carry):
+        load(chunk).wait()
         rows = pl.ds(pl.multiple_of(chunk * CHUNK, CHUNK), CHUNK)
         across = lax.broadcasted_iota(jnp.int32, (CHUNK, chans), 1)
         down = lax.broadcasted_iota(jnp.int32, (CHUNK, chans), 0) + chunk * CHUNK
         live = jnp.broadcast_to(mask_ref[...].astype(jnp.float32), (CHUNK, chans))
         mask = jnp.sum(jnp.where(across == down, live, 0.0), axis=1, keepdims=True)
-        mask = jnp.broadcast_to(mask, (CHUNK, LANES))
+        mask = jnp.broadcast_to(mask, (CHUNK, LANES)).astype(jnp.bfloat16)
 
         def one(tile, carry):
             columns = pl.ds(pl.multiple_of(tile * LANES, LANES), LANES)
-            held_signal[0, rows, columns] = (x_ref[rows, columns].astype(jnp.float32) * mask).astype(jnp.bfloat16)
+            held_signal[0, rows, columns] = x_ref[rows, columns] * mask
             return carry
 
         return lax.fori_loop(0, span // LANES, one, carry, unroll=8)
 
-    lax.fori_loop(0, chunks, mask_rows, 0)
+    load_mask.wait()
+    lax.fori_loop(0, 2, mask_rows, 0)
     pl.semaphore_wait(barrier, ranks - 1 + jnp.where(tm > 0, 1, 0) + jnp.where(tm < blocks - 1, 1, 0))
 
     def halo_copy(to):
@@ -142,22 +159,17 @@
         signal_copy(chunk).start()
         return carry
 
+    lax.fori_loop(0, 2, send_signal, 0)
+    lax.fori_loop(2, chunks, mask_rows, 0)
+
     @pl.when(tm > 0)
     def _():
         halo_copy(tm - 1).start()
 
-    lax.fori_loop(0, 2, send_signal, 0)
 
     @pl.when(tm == blocks - 1)
     def _():
         held_signal[:, :, span:] = jnp.zeros((2, chans, SEG), jnp.bfloat16)
-
-    for block in range(NP // LANES):
-        row = slow_ref[:, block * LANES:(block + 1) * LANES].astype(jnp.float32)
-        across = lax.broadcasted_iota(jnp.int32, (LANES, LANES), 1)
-        down = lax.broadcasted_iota(jnp.int32, (LANES, LANES), 0)
-        column = jnp.sum(jnp.where(across == down, jnp.broadcast_to(row, (LANES, LANES)), 0.0), axis=1, keepdims=True)
-        slow[block * LANES:(block + 1) * LANES, :] = jnp.broadcast_to(column, (LANES, LANES)).astype(jnp.int32)
 
     @pl.when(tm < blocks - 1)
     def _():
@@ -215,11 +227,22 @@
         lax.fori_loop(half + 1, ranks, launch, 0)
         recv[chunk, origin] = send[slot, chunk, pl.ds(lax.rem(me, half) * own, own)]
 
+    load_table.wait()
+    load_offsets.wait()
+    load_steps.wait()
+
     def own_spectra(chunk, carry):
         spectra(0, chunk, me)
         return carry
 
     lax.fori_loop(0, chunks, own_spectra, 0)
+
+    for block in range(NP // LANES):
+        row = slow_ref[:, block * LANES:(block + 1) * LANES].astype(jnp.float32)
+        across = lax.broadcasted_iota(jnp.int32, (LANES, LANES), 1)
+        down = lax.broadcasted_iota(jnp.int32, (LANES, LANES), 0)
+        column = jnp.sum(jnp.where(across == down, jnp.broadcast_to(row, (LANES, LANES)), 0.0), axis=1, keepdims=True)
+        slow[block * LANES:(block + 1) * LANES, :] = jnp.broadcast_to(column, (LANES, LANES)).astype(jnp.int32)
 
     def steering(step, carry):
         f, rows = step // (NP // ROWS), lax.rem(step, NP // ROWS) * ROWS
@@ -271,34 +294,31 @@
 
     others = pl.ds(0, ranks - 1)
 
-    def add(chunk, first, last):
+    def arrivals(chunk):
         held = recv.at[chunk, pl.ds(0, ranks - 2)]
         pltpu.make_async_copy(held, held, recv_sems.at[chunk]).wait()
+
+    def add(chunk, first):
+        arrivals(chunk)
 
         def one_bin(f, carry):
             spec = recv[chunk, :, f].reshape(width, 2 * segs)
             both = jnp.dot(steer[f, chunk], spec, preferred_element_type=jnp.float32)
             real = both[:NP, :segs] - both[NP:, segs:]
             imag = both[:NP, segs:] + both[NP:, :segs]
-            if not first:
-                real, imag = beam_ref[f, 0] + real, beam_ref[f, 1] + imag
-            beam_ref[f, 0] = real
-            beam_ref[f, 1] = imag
-            if last:
-                energy[...] += real * real + imag * imag
+            beam_ref[f, 0] = real if first else beam_ref[f, 0] + real
+            beam_ref[f, 1] = imag if first else beam_ref[f, 1] + imag
             return carry
 
         lax.fori_loop(0, own, one_bin, 0, unroll=8)
 
-    add(0, True, False)
+    add(0, True)
 
     def more(chunk, carry):
-        add(chunk, False, False)
+        add(chunk, False)
         return carry
 
     lax.fori_loop(1, chunks - 1, more, 0)
-    energy[...] = jnp.zeros((NP, segs), jnp.float32)
-    add(chunks - 1, False, True)
 
     def power_copy(to):
         return pltpu.make_async_remote_copy(
@@ -310,19 +330,40 @@
             device_id_type=pl.DeviceIdType.MESH,
         )
 
-    def power_of(to):
-        rows = pl.ds(pl.multiple_of(to * slows, slows), slows)
-
-        return energy[rows, :] * (1.0 / NF)
-
-    def power_term(d, carry):
-        to = peer(d)
-        terms[to] = power_of(to).astype(terms.dtype)
-        power_copy(to).start()
-        return carry
-
-    others_of(power_term)
-    arrived[me] = power_of(me).astype(arrived.dtype)
+    last = chunks - 1
+    rows_of_side = NP // 2
+    energy[...] = jnp.zeros((rows_of_side, segs), jnp.float32)
+    arrivals(last)
+
+    def finish_side(phase, carry):
+        owners = lax.rem(side + 1 + phase, 2)
+        base = pl.multiple_of(owners * rows_of_side, rows_of_side)
+        rows = pl.ds(base, rows_of_side)
+
+        def one_bin(f, acc):
+            spec = recv[last, :, f].reshape(width, 2 * segs)
+            both = jnp.concatenate([steer[f, last, pl.ds(base + part * NP, rows_of_side), :] for part in range(2)])
+            both = jnp.dot(both, spec, preferred_element_type=jnp.float32)
+            real = beam_ref[f, 0, rows, :] + (both[:rows_of_side, :segs] - both[rows_of_side:, segs:])
+            imag = beam_ref[f, 1, rows, :] + (both[:rows_of_side, segs:] + both[rows_of_side:, :segs])
+            beam_ref[f, 0, rows, :] = real
+            beam_ref[f, 1, rows, :] = imag
+            energy[...] = jnp.where(f == 0, 0.0, energy[...]) + (real * real + imag * imag)
+            return acc
+
+        lax.fori_loop(0, own, one_bin, 0, unroll=8)
+        mine = terms.at[pl.ds(owners * half, half)]
+        mine[...] = (energy[...] * (1.0 / NF)).reshape(half, slows, segs).astype(terms.dtype)
+
+        def power_term(d, carry):
+            power_copy(peer(half - 1 - d + phase * (ranks + 1))).start()
+            return carry
+
+        lax.fori_loop(phase * (half + 1), half + phase * half, power_term, 0)
+        return carry
+
+    lax.fori_loop(0, 2, finish_side, 0)
+    arrived[me] = terms[me]
     pltpu.make_async_copy(arrived.at[others], arrived.at[others], power_sems.at[1]).wait()
 
     def sum_up(r, acc):
@@ -361,9 +402,14 @@
             pltpu.VMEM((own, 2, NP, segs), jnp.float32),
             pltpu.VMEM((NP // ranks, segs), jnp.float32),
         ),
-        in_specs=[pl.BlockSpec(memory_space=pltpu.SMEM), vmem, vmem, vmem, vmem],
+        in_specs=[pl.BlockSpec(memory_space=pl.ANY)] * 5,
         out_specs=(vmem, vmem),
         scratch_shapes=[
+            pltpu.SMEM(offsets.shape, offsets.dtype),
+            pltpu.VMEM(mask.shape, mask.dtype),
+            pltpu.VMEM(table.shape, table.dtype),
+            pltpu.VMEM(slow.shape, slow.dtype),
+            pltpu.VMEM(signal.shape, signal.dtype),
             pltpu.VMEM((NP, LANES), jnp.int32),
             pltpu.VMEM((2, chans, signal.shape[1] + SEG), jnp.bfloat16),
         ]
@@ -373,7 +419,7 @@
             pltpu.VMEM((2, chunks, NF // 2, CHUNK, 2 * segs), jnp.bfloat16),
             pltpu.VMEM((chunks, ranks, own, CHUNK, 2 * segs), jnp.bfloat16),
             pltpu.VMEM((own, chunks, 2 * NP, ranks * CHUNK), jnp.bfloat16),
-            pltpu.VMEM((NP, segs), jnp.float32),
+            pltpu.VMEM((NP // 2, segs), jnp.float32),
             pltpu.VMEM((ranks, slows, segs), term),
             pltpu.VMEM((ranks, slows, segs), term),
             pltpu.SemaphoreType.DMA((2, chunks)),
@@ -384,6 +430,8 @@
             pltpu.SemaphoreType.DMA((chunks,)),
             pltpu.SemaphoreType.DMA((chunks,)),
             pltpu.SemaphoreType.DMA((chunks,)),
+            pltpu.SemaphoreType.DMA((chunks,)),
+            pltpu.SemaphoreType.DMA((4,)),
         ],
         compiler_params=pltpu.CompilerParams(vmem_limit_bytes=VMEM_LIMIT, collective_id=0, has_side_effects=True),
         cost_estimate=pl.CostEstimate(flops=7 << 30, bytes_accessed=8 << 20, transcendentals=0),

time: 103 us -> 102 us (level)
    pallas_call x1, Pallas kernels: 100 us -> 99 us  [fused(): pl.pallas_call(functools.partial(fused_kernel, ranks=ranks, blocks=blocks...]
where the time goes in v3:
time: 102 us
  Pallas kernels  101 us (99%)
    pallas_call x1, Pallas kernels, fused(): pl.pallas_call(functools.partial(fused_kernel, ranks=ranks, blocks=blocks...  99 us
    pallas_call x1, Pallas kernels, store(): pl.pallas_call(store_kernel, out_shape=(jax.ShapeDtypeStruct(beam.shape,...  2.08 us

profile of v3, /device:TPU:0, one launch (start us, length us, event | category | flops | bytes accessed | tf_op | source)
XLA Modules:
  0.0 101.8 jit_solution(8124505797315876948)
XLA Ops:
  0.6 99.0 %beamform.1 = (f32[8,2,512,128]{3,2,1,0:T(8,128)S(1)}, f32[32,128]{1,0:T(8,128)S(1)}) custom-call(s32[128]{0:T(128)} %offsets_ref.1, bf16[80,8192]{1,0:T(8,128)(2,1)} %signal_ref.1, s32[1,80]{1,0:T(1,128)} %bitcast.3, bf16[256,256]{1,0:T(8,128)(2,1)} %constant.2.clone.taper_ref, s32[1,512]{1,0:T(1,128)} %bitcast.2), custom_call_target="tpu_custom_call" | custom-call | flops 7516192768 | bytes 8388608 | tf_op jit(solution)/shard_map/beamform/pallas_call | solution.py:399
  99.7 2.1 %store.1 = (f32[8,2,512,128]{3,2,1,0:T(8,128)}, f32[32,128]{1,0:T(8,128)}) custom-call(f32[8,2,512,128]{3,2,1,0:T(8,128)S(1)} %get-tuple-element.4.beam_ref, f32[32,128]{1,0:T(8,128)S(1)} %get-tuple-element.5.power_ref), custom_call_target="tpu_custom_call" | custom-call | bytes 8388608 | tf_op jit(solution)/shard_map/store/pallas_call | solution.py:459

commit v4 on v3

--- a/solution.py
+++ b/solution.py
@@ -103,8 +103,9 @@
         rows = pl.ds(pl.multiple_of(chunk * CHUNK, CHUNK), CHUNK)
         return pltpu.make_async_copy(signal_ref.at[rows], x_ref.at[rows], load_sems.at[chunk])
 
-    def mask_rows(chunk, carry):
-        load(chunk).wait()
+    edge = SEG // LANES
+
+    def mask_tiles(chunk, low, high):
         rows = pl.ds(pl.multiple_of(chunk * CHUNK, CHUNK), CHUNK)
         across = lax.broadcasted_iota(jnp.int32, (CHUNK, chans), 1)
         down = lax.broadcasted_iota(jnp.int32, (CHUNK, chans), 0) + chunk * CHUNK
@@ -117,9 +118,19 @@
             held_signal[0, rows, columns] = x_ref[rows, columns] * mask
             return carry
 
-        return lax.fori_loop(0, span // LANES, one, carry, unroll=8)
+        lax.fori_loop(low, high, one, 0, unroll=(high - low) // 2)
+
+    def mask_edge(chunk, carry):
+        load(chunk).wait()
+        mask_tiles(chunk, 0, edge)
+        return carry
+
+    def mask_rows(chunk, carry):
+        mask_tiles(chunk, edge, span // LANES)
+        return carry
 
     load_mask.wait()
+    lax.fori_loop(0, chunks, mask_edge, 0)
     lax.fori_loop(0, 2, mask_rows, 0)
     pl.semaphore_wait(barrier, ranks - 1 + jnp.where(tm > 0, 1, 0) + jnp.where(tm < blocks - 1, 1, 0))
 
@@ -159,33 +170,30 @@
         signal_copy(chunk).start()
         return carry
 
-    lax.fori_loop(0, 2, send_signal, 0)
-    lax.fori_loop(2, chunks, mask_rows, 0)
-
     @pl.when(tm > 0)
     def _():
         halo_copy(tm - 1).start()
 
+    lax.fori_loop(0, 2, send_signal, 0)
+    lax.fori_loop(2, chunks, mask_rows, 0)
 
     @pl.when(tm == blocks - 1)
     def _():
         held_signal[:, :, span:] = jnp.zeros((2, chans, SEG), jnp.bfloat16)
-
-    @pl.when(tm < blocks - 1)
-    def _():
-        halo_copy(tm + 1).wait_recv()
 
     def block_copy(slot, chunk, origin, to):
         return pltpu.make_async_remote_copy(
             src_ref=send.at[slot, chunk, pl.ds(lax.rem(to, half) * own, own)],
             dst_ref=recv.at[chunk, origin],
             send_sem=send_sems.at[slot, chunk],
-            recv_sem=recv_sems.at[chunk],
+            recv_sem=recv_sems.at[slot, chunk],
             device_id={"chan": to},
             device_id_type=mesh_ids,
         )
 
-    def spectra(slot, chunk, origin):
+    inner = 2 * ((span - 3 * LANES) // LANES + 1)
+
+    def spectra(slot, chunk, origin, edge_ready):
         top = pl.multiple_of(chunk * CHUNK, CHUNK)
 
         def gather(s, carry):
@@ -198,7 +206,9 @@
             p1[pl.ds(s, CHUNK, stride=step), :] = jnp.where(keep, b, c)
             return carry
 
-        lax.fori_loop(0, segs, gather, 0, unroll=128)
+        lax.fori_loop(0, inner, gather, 0, unroll=124)
+        edge_ready()
+        lax.fori_loop(inner, segs, gather, 0, unroll=4)
         table = table_ref[pl.ds(pl.multiple_of(side * NF, NF), NF), :]
 
         def transform(i, carry):
@@ -232,7 +242,12 @@
     load_steps.wait()
 
     def own_spectra(chunk, carry):
-        spectra(0, chunk, me)
+        def edge_ready():
+            @pl.when((chunk == 0) & (tm < blocks - 1))
+            def _():
+                halo_copy(tm + 1).wait_recv()
+
+        spectra(0, chunk, me, edge_ready)
         return carry
 
     lax.fori_loop(0, chunks, own_spectra, 0)
@@ -282,11 +297,12 @@
         def _():
             edge_copy(chunk, tm - 1).start()
 
-        @pl.when(tm < blocks - 1)
-        def _():
-            edge_copy(chunk, tm + 1).wait_recv()
-
-        spectra(1, chunk, mirror)
+        def edge_ready():
+            @pl.when(tm < blocks - 1)
+            def _():
+                edge_copy(chunk, tm + 1).wait_recv()
+
+        spectra(1, chunk, mirror, edge_ready)
         return carry
 
     lax.fori_loop(0, chunks, mirror_spectra, 0)
@@ -294,12 +310,13 @@
 
     others = pl.ds(0, ranks - 1)
 
-    def arrivals(chunk):
-        held = recv.at[chunk, pl.ds(0, ranks - 2)]
-        pltpu.make_async_copy(held, held, recv_sems.at[chunk]).wait()
+    def arrivals(slot, chunk):
+        held = recv.at[chunk, pl.ds(0, half - 1)]
+        pltpu.make_async_copy(held, held, recv_sems.at[slot, chunk]).wait()
 
     def add(chunk, first):
-        arrivals(chunk)
+        arrivals(0, chunk)
+        arrivals(1, chunk)
 
         def one_bin(f, carry):
             spec = recv[chunk, :, f].reshape(width, 2 * segs)
@@ -333,7 +350,25 @@
     last = chunks - 1
     rows_of_side = NP // 2
     energy[...] = jnp.zeros((rows_of_side, segs), jnp.float32)
-    arrivals(last)
+
+    def half_sum(f, group, base, count):
+        columns = pl.ds(pl.multiple_of(group * (width // 2), width // 2), width // 2)
+        steps = [steer[f, last, pl.ds(base + part * NP, count), columns] for part in range(2)]
+        spec = recv[last, pl.ds(group * half, half), f].reshape(width // 2, 2 * segs)
+        turned = jnp.concatenate([-spec[:, segs:], spec[:, :segs]], axis=1)
+        both = jnp.dot(jnp.concatenate(steps, axis=1), jnp.concatenate([spec, turned]), preferred_element_type=jnp.float32)
+        return both[:, :segs], both[:, segs:]
+
+    arrivals(0, last)
+
+    def own_half(f, carry):
+        real, imag = half_sum(f, side, 0, NP)
+        beam_ref[f, 0] += real
+        beam_ref[f, 1] += imag
+        return carry
+
+    lax.fori_loop(0, own, own_half, 0, unroll=8)
+    arrivals(1, last)
 
     def finish_side(phase, carry):
         owners = lax.rem(side + 1 + phase, 2)
@@ -341,11 +376,8 @@
         rows = pl.ds(base, rows_of_side)
 
         def one_bin(f, acc):
-            spec = recv[last, :, f].reshape(width, 2 * segs)
-            both = jnp.concatenate([steer[f, last, pl.ds(base + part * NP, rows_of_side), :] for part in range(2)])
-            both = jnp.dot(both, spec, preferred_element_type=jnp.float32)
-            real = beam_ref[f, 0, rows, :] + (both[:rows_of_side, :segs] - both[rows_of_side:, segs:])
-            imag = beam_ref[f, 1, rows, :] + (both[:rows_of_side, segs:] + both[rows_of_side:, :segs])
+            real, imag = half_sum(f, 1 - side, base, rows_of_side)
+            real, imag = beam_ref[f, 0, rows, :] + real, beam_ref[f, 1, rows, :] + imag
             beam_ref[f, 0, rows, :] = real
             beam_ref[f, 1, rows, :] = imag
             energy[...] = jnp.where(f == 0, 0.0, energy[...]) + (real * real + imag * imag)
@@ -369,7 +401,7 @@
     def sum_up(r, acc):
         return acc + arrived[r].astype(jnp.float32)
 
-    power_ref[...] = lax.fori_loop(0, ranks, sum_up, jnp.zeros((slows, segs), jnp.float32))
+    power_ref[...] = lax.fori_loop(0, ranks, sum_up, jnp.zeros((slows, segs), jnp.float32), unroll=16)
 
     def finish(chunk, carry):
         sent = recv.at[chunk, pl.ds(0, half - 1)]
@@ -423,7 +455,7 @@
             pltpu.VMEM((ranks, slows, segs), term),
             pltpu.VMEM((ranks, slows, segs), term),
             pltpu.SemaphoreType.DMA((2, chunks)),
-            pltpu.SemaphoreType.DMA((chunks,)),
+            pltpu.SemaphoreType.DMA((2, chunks)),
             pltpu.SemaphoreType.DMA((2,)),
             pltpu.SemaphoreType.DMA((2,)),
             pltpu.SemaphoreType.DMA((chunks,)),

time: 102 us -> 101 us (level)
  no operation moved by 1% of the time
where the time goes in v4:
time: 101 us
  Pallas kernels  100 us (99%)
    pallas_call x1, Pallas kernels, fused(): pl.pallas_call(functools.partial(fused_kernel, ranks=ranks, blocks=blocks...  98.1 us
    pallas_call x1, Pallas kernels, store(): pl.pallas_call(store_kernel, out_shape=(jax.ShapeDtypeStruct(beam.shape,...  2.08 us

profile of v4, /device:TPU:0, one launch (start us, length us, event | category | flops | bytes accessed | tf_op | source)
XLA Modules:
  0.0 100.9 jit_solution(16967695747475699795)
XLA Ops:
  0.6 98.1 %beamform.1 = (f32[8,2,512,128]{3,2,1,0:T(8,128)S(1)}, f32[32,128]{1,0:T(8,128)S(1)}) custom-call(s32[128]{0:T(128)} %offsets_ref.1, bf16[80,8192]{1,0:T(8,128)(2,1)} %signal_ref.1, s32[1,80]{1,0:T(1,128)} %bitcast.3, bf16[256,256]{1,0:T(8,128)(2,1)} %constant.2.clone.taper_ref, s32[1,512]{1,0:T(1,128)} %bitcast.2), custom_call_target="tpu_custom_call" | custom-call | flops 7516192768 | bytes 8388608 | tf_op jit(solution)/shard_map/beamform/pallas_call | solution.py:431
  98.8 2.1 %store.1 = (f32[8,2,512,128]{3,2,1,0:T(8,128)}, f32[32,128]{1,0:T(8,128)}) custom-call(f32[8,2,512,128]{3,2,1,0:T(8,128)S(1)} %get-tuple-element.4.beam_ref, f32[32,128]{1,0:T(8,128)S(1)} %get-tuple-element.5.power_ref), custom_call_target="tpu_custom_call" | custom-call | bytes 8388608 | tf_op jit(solution)/shard_map/store/pallas_call | solution.py:491

commit v5 on v4

--- a/solution.py
+++ b/solution.py
@@ -70,6 +70,24 @@
     barrier = pltpu.get_barrier_semaphore()
     mesh_ids = pl.DeviceIdType.MESH
 
+    def greet(d, carry):
+        pl.semaphore_signal(barrier, inc=1, device_id={"chan": peer(d)}, device_id_type=mesh_ids)
+        return carry
+
+    def others_of(body):
+        lax.fori_loop(0, half, body, 0, unroll=8)
+        lax.fori_loop(half + 1, ranks, body, 0, unroll=min(7, half - 1))
+
+    @pl.when(tm > 0)
+    def _():
+        pl.semaphore_signal(barrier, inc=1, device_id={"tm": tm - 1}, device_id_type=mesh_ids)
+
+    @pl.when(tm < blocks - 1)
+    def _():
+        pl.semaphore_signal(barrier, inc=1, device_id={"tm": tm + 1}, device_id_type=mesh_ids)
+
+    others_of(greet)
+
     smalls = ((channel_mask_ref, mask_ref), (taper_ref, table_ref), (offsets_ref, offs), (steps_ref, slow_ref))
     load_mask, load_table, load_offsets, load_steps = [pltpu.make_async_copy(*pair, small_sems.at[i]) for i, pair in enumerate(smalls)]
     load_mask.start()
@@ -80,24 +98,6 @@
     load_table.start()
     load_offsets.start()
     load_steps.start()
-
-    def greet(d, carry):
-        pl.semaphore_signal(barrier, inc=1, device_id={"chan": peer(d)}, device_id_type=mesh_ids)
-        return carry
-
-    def others_of(body):
-        lax.fori_loop(0, half, body, 0, unroll=8)
-        lax.fori_loop(half + 1, ranks, body, 0, unroll=min(7, half - 1))
-
-    @pl.when(tm > 0)
-    def _():
-        pl.semaphore_signal(barrier, inc=1, device_id={"tm": tm - 1}, device_id_type=mesh_ids)
-
-    @pl.when(tm < blocks - 1)
-    def _():
-        pl.semaphore_signal(barrier, inc=1, device_id={"tm": tm + 1}, device_id_type=mesh_ids)
-
-    others_of(greet)
 
     def load(chunk):
         rows = pl.ds(pl.multiple_of(chunk * CHUNK, CHUNK), CHUNK)
@@ -396,12 +396,6 @@
 
     lax.fori_loop(0, 2, finish_side, 0)
     arrived[me] = terms[me]
-    pltpu.make_async_copy(arrived.at[others], arrived.at[others], power_sems.at[1]).wait()
-
-    def sum_up(r, acc):
-        return acc + arrived[r].astype(jnp.float32)
-
-    power_ref[...] = lax.fori_loop(0, ranks, sum_up, jnp.zeros((slows, segs), jnp.float32), unroll=16)
 
     def finish(chunk, carry):
         sent = recv.at[chunk, pl.ds(0, half - 1)]
@@ -415,11 +409,19 @@
         return carry
 
     lax.fori_loop(0, chunks, finish, 0)
-    pltpu.make_async_copy(terms.at[others], terms.at[others], power_sems.at[0]).wait()
 
     @pl.when(tm > 0)
     def _():
         halo_copy(tm - 1).wait_send()
+
+    pltpu.make_async_copy(arrived.at[others], arrived.at[others], power_sems.at[1]).wait()
+
+    def sum_up(r, acc):
+        return acc + arrived[r].astype(jnp.float32)
+
+    power_ref[...] = lax.fori_loop(0, ranks, sum_up, jnp.zeros((slows, segs), jnp.float32), unroll=16)
+
+    pltpu.make_async_copy(terms.at[others], terms.at[others], power_sems.at[0]).wait()
 
 
 def fused(signal, mask, offsets, table, slow, ranks, blocks):

time: 101 us -> 101 us (level)
  no operation moved by 1% of the time
where the time goes in v5:
time: 101 us
  Pallas kernels  100 us (99%)
    pallas_call x1, Pallas kernels, fused(): pl.pallas_call(functools.partial(fused_kernel, ranks=ranks, blocks=blocks...  98.1 us
    pallas_call x1, Pallas kernels, store(): pl.pallas_call(store_kernel, out_shape=(jax.ShapeDtypeStruct(beam.shape,...  2.08 us

profile of v5, /device:TPU:0, one launch (start us, length us, event | category | flops | bytes accessed | tf_op | source)
XLA Modules:
  0.0 100.8 jit_solution(7908719227912810493)
XLA Ops:
  0.6 98.1 %beamform.1 = (f32[8,2,512,128]{3,2,1,0:T(8,128)S(1)}, f32[32,128]{1,0:T(8,128)S(1)}) custom-call(s32[128]{0:T(128)} %offsets_ref.1, bf16[80,8192]{1,0:T(8,128)(2,1)} %signal_ref.1, s32[1,80]{1,0:T(1,128)} %bitcast.3, bf16[256,256]{1,0:T(8,128)(2,1)} %constant.2.clone.taper_ref, s32[1,512]{1,0:T(1,128)} %bitcast.2), custom_call_target="tpu_custom_call" | custom-call | flops 7516192768 | bytes 8388608 | tf_op jit(solution)/shard_map/beamform/pallas_call | solution.py:433
  98.7 2.1 %store.1 = (f32[8,2,512,128]{3,2,1,0:T(8,128)}, f32[32,128]{1,0:T(8,128)}) custom-call(f32[8,2,512,128]{3,2,1,0:T(8,128)S(1)} %get-tuple-element.4.beam_ref, f32[32,128]{1,0:T(8,128)S(1)} %get-tuple-element.5.power_ref), custom_call_target="tpu_custom_call" | custom-call | bytes 8388608 | tf_op jit(solution)/shard_map/store/pallas_call | solution.py:493

commit v6 on v5

--- a/solution.py
+++ b/solution.py
@@ -335,7 +335,27 @@
         add(chunk, False)
         return carry
 
-    lax.fori_loop(1, chunks - 1, more, 0)
+    lax.fori_loop(1, chunks - 2, more, 0)
+    last = chunks - 1
+
+    def half_sum(f, group, base, count):
+        columns = pl.ds(pl.multiple_of(group * (width // 2), width // 2), width // 2)
+        steps = [steer[f, last, pl.ds(base + part * NP, count), columns] for part in range(2)]
+        spec = recv[last, pl.ds(group * half, half), f].reshape(width // 2, 2 * segs)
+        turned = jnp.concatenate([-spec[:, segs:], spec[:, :segs]], axis=1)
+        both = jnp.dot(jnp.concatenate(steps, axis=1), jnp.concatenate([spec, turned]), preferred_element_type=jnp.float32)
+        return both[:, :segs], both[:, segs:]
+
+    arrivals(0, last)
+
+    def own_half(f, carry):
+        real, imag = half_sum(f, side, 0, NP)
+        beam_ref[f, 0] += real
+        beam_ref[f, 1] += imag
+        return carry
+
+    lax.fori_loop(0, own, own_half, 0, unroll=8)
+    add(chunks - 2, False)
 
     def power_copy(to):
         return pltpu.make_async_remote_copy(
@@ -347,27 +367,9 @@
             device_id_type=pl.DeviceIdType.MESH,
         )
 
-    last = chunks - 1
     rows_of_side = NP // 2
     energy[...] = jnp.zeros((rows_of_side, segs), jnp.float32)
 
-    def half_sum(f, group, base, count):
-        columns = pl.ds(pl.multiple_of(group * (width // 2), width // 2), width // 2)
-        steps = [steer[f, last, pl.ds(base + part * NP, count), columns] for part in range(2)]
-        spec = recv[last, pl.ds(group * half, half), f].reshape(width // 2, 2 * segs)
-        turned = jnp.concatenate([-spec[:, segs:], spec[:, :segs]], axis=1)
-        both = jnp.dot(jnp.concatenate(steps, axis=1), jnp.concatenate([spec, turned]), preferred_element_type=jnp.float32)
-        return both[:, :segs], both[:, segs:]
-
-    arrivals(0, last)
-
-    def own_half(f, carry):
-        real, imag = half_sum(f, side, 0, NP)
-        beam_ref[f, 0] += real
-        beam_ref[f, 1] += imag
-        return carry
-
-    lax.fori_loop(0, own, own_half, 0, unroll=8)
     arrivals(1, last)
 
     def finish_side(phase, carry):

time: 101 us -> 101 us (level)
  no operation moved by 1% of the time
where the time goes in v6:
time: 101 us
  Pallas kernels  100 us (99%)
    pallas_call x1, Pallas kernels, fused(): pl.pallas_call(functools.partial(fused_kernel, ranks=ranks, blocks=blocks...  98.1 us
    pallas_call x1, Pallas kernels, store(): pl.pallas_call(store_kernel, out_shape=(jax.ShapeDtypeStruct(beam.shape,...  2.08 us

profile of v6, /device:TPU:0, one launch (start us, length us, event | category | flops | bytes accessed | tf_op | source)
XLA Modules:
  0.0 100.8 jit_solution(7849886822689520463)
XLA Ops:
  0.6 98.1 %beamform.1 = (f32[8,2,512,128]{3,2,1,0:T(8,128)S(1)}, f32[32,128]{1,0:T(8,128)S(1)}) custom-call(s32[128]{0:T(128)} %offsets_ref.1, bf16[80,8192]{1,0:T(8,128)(2,1)} %signal_ref.1, s32[1,80]{1,0:T(1,128)} %bitcast.3, bf16[256,256]{1,0:T(8,128)(2,1)} %constant.2.clone.taper_ref, s32[1,512]{1,0:T(1,128)} %bitcast.2), custom_call_target="tpu_custom_call" | custom-call | flops 7516192768 | bytes 8388608 | tf_op jit(solution)/shard_map/beamform/pallas_call | solution.py:435
  98.7 2.1 %store.1 = (f32[8,2,512,128]{3,2,1,0:T(8,128)}, f32[32,128]{1,0:T(8,128)}) custom-call(f32[8,2,512,128]{3,2,1,0:T(8,128)S(1)} %get-tuple-element.4.beam_ref, f32[32,128]{1,0:T(8,128)S(1)} %get-tuple-element.5.power_ref), custom_call_target="tpu_custom_call" | custom-call | bytes 8388608 | tf_op jit(solution)/shard_map/store/pallas_call | solution.py:495

commit v7 on v5

--- a/solution.py
+++ b/solution.py
@@ -131,7 +131,7 @@
 
     load_mask.wait()
     lax.fori_loop(0, chunks, mask_edge, 0)
-    lax.fori_loop(0, 2, mask_rows, 0)
+    lax.fori_loop(0, 3, mask_rows, 0)
     pl.semaphore_wait(barrier, ranks - 1 + jnp.where(tm > 0, 1, 0) + jnp.where(tm < blocks - 1, 1, 0))
 
     def halo_copy(to):
@@ -174,8 +174,8 @@
     def _():
         halo_copy(tm - 1).start()
 
-    lax.fori_loop(0, 2, send_signal, 0)
-    lax.fori_loop(2, chunks, mask_rows, 0)
+    lax.fori_loop(0, 3, send_signal, 0)
+    lax.fori_loop(3, chunks, mask_rows, 0)
 
     @pl.when(tm == blocks - 1)
     def _():
@@ -287,9 +287,9 @@
         lax.fori_loop(steps * chunk // (2 * chunks), steps * (chunk + 1) // (2 * chunks), steering, 0)
         signal_copy(chunk).wait_send()
 
-        @pl.when(chunk + 2 < chunks)
+        @pl.when(chunk + 3 < chunks)
         def _():
-            signal_copy(chunk + 2).start()
+            signal_copy(chunk + 3).start()
 
         signal_copy(chunk).wait_recv()
 

time: 101 us -> 101 us (level)
  no operation moved by 1% of the time
where the time goes in v7:
time: 101 us
  Pallas kernels  100 us (99%)
    pallas_call x1, Pallas kernels, fused(): pl.pallas_call(functools.partial(fused_kernel, ranks=ranks, blocks=blocks...  97.9 us
    pallas_call x1, Pallas kernels, store(): pl.pallas_call(store_kernel, out_shape=(jax.ShapeDtypeStruct(beam.shape,...  2.08 us

profile of v7, /device:TPU:0, one launch (start us, length us, event | category | flops | bytes accessed | tf_op | source)
XLA Modules:
  0.0 100.6 jit_solution(16165009958073732525)
XLA Ops:
  0.6 97.9 %beamform.1 = (f32[8,2,512,128]{3,2,1,0:T(8,128)S(1)}, f32[32,128]{1,0:T(8,128)S(1)}) custom-call(s32[128]{0:T(128)} %offsets_ref.1, bf16[80,8192]{1,0:T(8,128)(2,1)} %signal_ref.1, s32[1,80]{1,0:T(1,128)} %bitcast.3, bf16[256,256]{1,0:T(8,128)(2,1)} %constant.2.clone.taper_ref, s32[1,512]{1,0:T(1,128)} %bitcast.2), custom_call_target="tpu_custom_call" | custom-call | flops 7516192768 | bytes 8388608 | tf_op jit(solution)/shard_map/beamform/pallas_call | solution.py:433
  98.5 2.1 %store.1 = (f32[8,2,512,128]{3,2,1,0:T(8,128)}, f32[32,128]{1,0:T(8,128)}) custom-call(f32[8,2,512,128]{3,2,1,0:T(8,128)S(1)} %get-tuple-element.4.beam_ref, f32[32,128]{1,0:T(8,128)S(1)} %get-tuple-element.5.power_ref), custom_call_target="tpu_custom_call" | custom-call | bytes 8388608 | tf_op jit(solution)/shard_map/store/pallas_call | solution.py:493
